TPU v7x, 32 devices: a whole 2x2x4 slice. The times are simulated.
32 devices in a mesh: gx: 8 (over y, x, core), gy: 4 (over z).
Axes of the slice: x: 2, y: 2, z: 4, core: 2. Of those that a mesh axis runs over, the one named last changes fastest.
Arguments:
- spectra: float32 [16, 4, 33, 4, 512], P('gx', None, None, None, 'gy'), may hold values from 0.05 to 2
- collection: float32 [4, 33, 561], replicated, may hold values from -0.125 to 0.125
- growth_rate: float32 [4, 33], replicated, may hold values from 0.1 to 1
- fall_speed: float32 [4, 33], replicated, may hold values from 0.05 to 0.9
- supersaturation: float32 [16, 4, 512], P('gx', None, 'gy'), may hold values from -0.4 to 0.4
- courant: float32 [16, 4, 512], P('gx', None, 'gy'), may hold values from -0.8 to 0.8
- cloudy: int32 [16, 512], P('gx', 'gy'), may hold values from 0 to 1, as said below
Outputs:
- spectra_out: float32 [16, 4, 33, 4, 512], P('gx', None, None, None, 'gy')
Inputs may be any that keep to these rules, and one draw needn't show every extreme that they name: A block is the 128 columns of one x-row that lie on one device; each device holds 2 blocks, and a block is cloudy if any of its entries is 1. In every aligned run of 8 devices along gx with one gy index at most 8 blocks are cloudy; in every draw some run has exactly that many, and some device has all 2 of its blocks cloudy.
All inputs are finite; a program needn't handle non-finite values.
Results may differ from a plain program's by a relative error of at most 0.0003.
Values sent between devices are 32-bit elements; how exact they have to be, the bound alone decides.
A program may use at most 64 MiB of HBM per device.

v0:
```python
import functools

import jax
import jax.numpy as jnp
from jax import lax
from jax.experimental import pallas as pl
from jax.experimental.pallas import tpu as pltpu
from jax.sharding import PartitionSpec as P

SUB = 2
LANES = 128
CHUNK = 4
F32 = jnp.float32
BF16 = jnp.bfloat16


def rounded(x):
    return x.astype(BF16).astype(F32)


def kernel(
    dims,
    f_ref,
    coll_ref,
    rate_ref,
    fall_ref,
    sat_ref,
    cour_ref,
    cloudy_ref,
    out_ref,
    cm,
    k_last,
    tail,
    cells,
    gs,
    edge,
    from_left,
    from_right,
    send_sem,
    recv_sem,
):
    blocks, types, bins, levels, cols, n_y = dims
    low = bins // 8 * 8
    rows = low + 8
    per_type = blocks * levels
    groups = types * per_type
    me = lax.axis_index("gy")
    right, left = lax.rem(me + 1, n_y), lax.rem(me + n_y - 1, n_y)
    mesh_id = pl.DeviceIdType.MESH
    barrier = pltpu.get_barrier_semaphore()
    for peer in (left, right):
        pl.semaphore_signal(barrier, inc=1, device_id={"gy": peer}, device_id_type=mesh_id)

    lane = lax.broadcasted_iota(jnp.int32, (rows, LANES), 1)
    sub = lax.broadcasted_iota(jnp.int32, (rows, LANES), 0)

    edge[...] = jnp.zeros_like(edge)
    for t in range(types):
        for b in range(blocks):
            for v in range(levels):
                g = (t * blocks + b) * levels + v
                base = ((b * types + t) * bins) * levels + v
                cells[g, bins:rows] = jnp.zeros((rows - bins, cols), F32)
                cells[g, 0:bins] = f_ref[pl.ds(base, bins, stride=levels), :]
                cells[g, bins : bins + 1] = cour_ref[b, v : v + 1, :]
                cells[g, bins + 1 : bins + 2] = sat_ref[b, v : v + 1, :]
                cells[g, bins + 2 : bins + 3] = cloudy_ref[b : b + 1, :].astype(F32)
    packed = jnp.zeros((rows, LANES), F32)
    for g in range(groups):
        packed = jnp.where(
            (lane >= 4 * g) & (lane < 4 * g + 4),
            pltpu.roll(cells[g], (4 * g + 2) % LANES, 1),
            packed,
        )
    edge[...] = packed

    pl.semaphore_wait(barrier, 2)
    copies = []
    for index, (peer, landing) in enumerate(((right, from_left), (left, from_right))):
        copy = pltpu.make_async_remote_copy(
            src_ref=edge,
            dst_ref=landing,
            send_sem=send_sem.at[index],
            recv_sem=recv_sem.at[index],
            device_id={"gy": peer},
            device_id_type=mesh_id,
        )
        copy.start()
        copies.append(copy)

    def column(ref, t):
        row = jnp.broadcast_to(ref[t : t + 1, :], (rows, bins))
        r = lax.broadcasted_iota(jnp.int32, (rows, bins), 0)
        c = lax.broadcasted_iota(jnp.int32, (rows, bins), 1)
        return jnp.sum(jnp.where(r == c, row, 0.0), axis=1, keepdims=True)

    rates = [jnp.broadcast_to(column(rate_ref, t), (rows, LANES)) for t in range(types)]
    falls = [jnp.broadcast_to(column(fall_ref, t), (rows, LANES)) for t in range(types)]

    pairs = coll_ref.shape[2]
    whole = pairs // LANES
    lane_b = lax.broadcasted_iota(jnp.int32, (bins, LANES), 1)
    for t in range(types):
        tail[...] = jnp.zeros_like(tail)
        if pairs % LANES:
            tail[0:bins, 0 : pairs - whole * LANES] = coll_ref[t, :, whole * LANES : pairs]
        k_last[...] = jnp.zeros_like(k_last)

        def tile(a):
            if a < whole:
                return coll_ref[t, :, a * LANES : (a + 1) * LANES]
            return tail[0:bins]

        first = 0
        for i in range(bins):
            count = bins - i
            a, end = first // LANES, (first + count - 1) // LANES
            shift = (i - first) % LANES
            x = pltpu.roll(tile(a), shift, 1) if shift else tile(a)
            if end > a:
                split = i + (a + 1) * LANES - first
                y = pltpu.roll(tile(end), shift, 1) if shift else tile(end)
                x = jnp.where(lane_b < split, x, y)
            x = jnp.where((lane_b >= i) & (lane_b < bins), x, 0.0)
            hi = rounded(x)
            stack = hi + pltpu.roll(x - hi, rows, 1) + pltpu.roll(hi, 2 * rows, 1)
            cm[t, i * low : (i + 1) * low] = stack[0:low].astype(BF16)
            k_last[i : i + 1] = stack[low:bins]
            first += count
        cm[t, bins * low :] = k_last[...].astype(BF16)

    def condense(f, r, sat):
        fr = r * f
        top = lax.broadcasted_iota(jnp.int32, f.shape, 0) < bins - 1
        up = jnp.where(top, fr, 0.0)
        rise = pltpu.roll(up, 1, 0) - up
        fall = pltpu.roll(fr, rows - 1, 0) - fr
        return f + jnp.maximum(sat, 0.0) * rise + jnp.maximum(-sat, 0.0) * fall

    def collide(t, g):
        width = g.shape[1]
        slot = gs.at[:, 0:width]
        slot[...] = g
        hi = rounded(g)
        stack = jnp.concatenate(
            [hi, hi, g - hi, jnp.zeros((LANES - 3 * rows, width), F32)], axis=0
        ).astype(BF16)
        acc = g[0:low]
        for start in range(0, bins, CHUNK):
            stop = min(start + CHUNK, bins)
            h = jnp.dot(cm[t, start * low : stop * low], stack, preferred_element_type=F32)
            for i in range(start, stop):
                acc = acc + slot[i : i + 1, :] * h[(i - start) * low : (i - start + 1) * low]
        h = jnp.dot(cm[t, bins * low :], stack, preferred_element_type=F32)
        last = jnp.sum(g * h[0:rows], axis=0, keepdims=True)
        rest = g[low:rows]
        rest = jnp.where(lax.broadcasted_iota(jnp.int32, rest.shape, 0) == 0, rest + last, rest)
        return jnp.concatenate([acc, rest], axis=0)

    def two(x, times):
        return jnp.concatenate([x] * times, axis=1) if times > 1 else x

    per = 2 if levels % 2 == 0 else 1
    for t in range(types):

        def one_block(b, carry, t=t):
            base = (t * blocks + b) * levels
            wet = []
            for v in range(0, levels, per):
                f = jnp.concatenate([cells[base + v + p] for p in range(per)], axis=1)
                g = condense(f, two(rates[t], per), f[bins + 1 : bins + 2])
                for _ in range(SUB):
                    g = collide(t, g)
                w = jnp.where(f[bins + 2 : bins + 3] > 0, g, f)
                wet += [w[:, p * LANES : (p + 1) * LANES] for p in range(per)]
            for v in range(levels):
                above = wet[v + 1] if v + 1 < levels else jnp.zeros_like(wet[v])
                cells[base + v] = wet[v] + falls[t] * (above - wet[v])
            return carry

        lax.fori_loop(0, blocks, one_block, 0)

    for copy in copies:
        copy.wait()
    f = jnp.where(lane % 4 < 2, from_left[...], from_right[...])
    kind = lane // (4 * per_type)
    r, v_fall = rates[0], falls[0]
    for t in range(1, types):
        r = jnp.where(kind == t, rates[t], r)
        v_fall = jnp.where(kind == t, falls[t], v_fall)
    g = condense(f, r, f[bins + 1 : bins + 2])
    for _ in range(SUB):
        new = collide(0, g)
        for t in range(1, types):
            new = jnp.where(kind == t, collide(t, g), new)
        g = new
    w = jnp.where(f[bins + 2 : bins + 3] > 0, g, f)
    above = jnp.where(lane // 4 % levels == levels - 1, 0.0, pltpu.roll(w, LANES - 4, 1))
    ghost = w + v_fall * (above - w)
    edge[...] = ghost

    def shifted(g, x, width_lane):
        near = pltpu.roll(edge[...], (cols - 2 - 4 * g) % LANES, 1)
        m2 = pltpu.roll(jnp.where(width_lane >= cols - 2, near, x), 2, 1)
        m1 = pltpu.roll(jnp.where(width_lane == cols - 1, near, x), 1, 1)
        p1 = pltpu.roll(jnp.where(width_lane == 0, near, x), LANES - 1, 1)
        p2 = pltpu.roll(jnp.where(width_lane < 2, near, x), LANES - 2, 1)
        return m2, m1, p1, p2

    for b in range(blocks):
        for v in range(levels):
            coef = None
            for t in range(types):
                g = (t * blocks + b) * levels + v
                x = cells[g]
                m2, m1, p1, p2 = shifted(g, x, lane)
                if coef is None:
                    c = 0.5 * (x[bins : bins + 1] + p1[bins : bins + 1])
                    d = 0.5 * (x[bins : bins + 1] + m1[bins : bins + 1])
                    ca, da = jnp.abs(c), jnp.abs(d)
                    coef = [
                        jnp.broadcast_to(e * (1.0 / 12.0), (rows, LANES))
                        for e in (
                            da - d,
                            7.0 * d - 3.0 * da - (ca - c),
                            7.0 * d + 3.0 * da - (7.0 * c - 3.0 * ca),
                            -d - da - (7.0 * c + 3.0 * ca),
                            c + ca,
                        )
                    ]
                y = x + coef[2] * x + coef[0] * m2 + coef[1] * m1 + coef[3] * p1 + coef[4] * p2
                base = ((b * types + t) * bins) * levels + v
                out_ref[pl.ds(base, bins, stride=levels), :] = y[0:bins]


def body(n_y, spectra, collection, growth_rate, fall_speed, supersaturation, courant, cloudy):
    blocks, types, bins, levels, cols = spectra.shape
    dims = (blocks, types, bins, levels, cols, n_y)
    low = bins // 8 * 8
    rows = low + 8
    total = blocks * types * bins * levels
    last = -(-rows // 16) * 16
    vmem = pl.BlockSpec(memory_space=pltpu.VMEM)
    out = pl.pallas_call(
        functools.partial(kernel, dims),
        out_shape=jax.ShapeDtypeStruct((total, cols), F32),
        in_specs=[vmem] * 7,
        out_specs=vmem,
        scratch_shapes=[
            pltpu.VMEM((types, bins * low + last, LANES), BF16),
            pltpu.VMEM((last, LANES), F32),
            pltpu.VMEM((rows, LANES), F32),
            pltpu.VMEM((blocks * types * levels, rows, cols), F32),
            pltpu.VMEM((rows, 2 * cols), F32),
            pltpu.VMEM((rows, LANES), F32),
            pltpu.VMEM((rows, LANES), F32),
            pltpu.VMEM((rows, LANES), F32),
            pltpu.SemaphoreType.DMA((2,)),
            pltpu.SemaphoreType.DMA((2,)),
        ],
        compiler_params=pltpu.CompilerParams(
            collective_id=0, has_side_effects=True, vmem_limit_bytes=32 * 2**20
        ),
    )(
        spectra.reshape(total, cols),
        collection,
        growth_rate,
        fall_speed,
        supersaturation,
        courant,
        cloudy,
    )
    return out.reshape(spectra.shape)


def solution(mesh):
    return jax.shard_map(
        functools.partial(body, mesh.shape["gy"]),
        mesh=mesh,
        in_specs=(
            P("gx", None, None, None, "gy"),
            P(),
            P(),
            P(),
            P("gx", None, "gy"),
            P("gx", None, "gy"),
            P("gx", "gy"),
        ),
        out_specs=P("gx", None, None, None, "gy"),
        check_vma=False,
    )
```

profile of v0, /device:TPU:0, one launch (start us, length us, event | category | flops | bytes accessed | tf_op | source)
XLA Modules:
  0.0 28.2 jit_solution(17907012742420978377)
XLA Ops:
  0.0 0.0 copy-start
  0.0 0.0 copy-start.1
  0.0 0.0 copy-start.2
  0.0 0.0 copy-start.3
  0.0 0.0 copy-start.4
  0.0 0.0 copy-start.5
  0.0 1.1 %copy.8.coll_ref = f32[4,33,561]{2,1,0:T(8,128)S(1)} copy(f32[4,33,561]{2,0,1:T(4,128)} %param.8) | data formatting | bytes 592416 | tf_op args[1]
  1.1 0.1 copy-done
  1.1 0.0 copy-done.1
  1.2 0.0 copy-done.2
  1.2 0.0 copy-done.3
  1.2 0.0 copy-done.4
  1.2 0.0 copy-done.5
  1.2 26.2 %shard_map.73 = f32[1056,128]{1,0:T(8,128)S(1)} custom-call(f32[1056,128]{1,0:T(8,128)S(1)} %bitcast.3, f32[4,33,561]{2,1,0:T(8,128)S(1)} %copy.8.coll_ref, f32[4,33]{1,0:T(4,128)S(1)} %copy-done.3, f32[4,33]{1,0:T(4,128)S(1)} %copy-done.4, f32[2,4,128]{2,1,0:T(4,128)S(1)} %copy-done.1, f32[2,4,128]{2,1,0:T(4,128)S(1)} %copy-done.2, s32[2,128]{1,0:T(2,128)S(1)} %copy-done.5), custom_call_target="tpu_custom_call" | custom-call | tf_op jit(solution)/shard_map/pallas_call | solution.py:244
  27.4 0.8 %copy.10 = f32[2,4,33,4,128]{4,3,2,1,0:T(4,128)} copy(f32[2,4,33,4,128]{4,3,2,1,0:T(4,128)S(1)} %bitcast.2) | data formatting | bytes 1081344
Async XLA Ops:
  0.0 1.1 %copy-start = (f32[2,4,33,4,128]{4,3,2,1,0:T(4,128)S(1)}, f32[2,4,33,4,128]{4,3,2,1,0:T(4,128)}, u32[]{:S(2)}) copy-start(f32[2,4,33,4,128]{4,3,2,1,0:T(4,128)} %param.7) | copy-start | bytes 1622020
  0.0 1.1 %copy-start.1 = (f32[2,4,128]{2,1,0:T(4,128)S(1)}, f32[2,4,128]{2,1,0:T(4,128)}, u32[]{:S(2)}) copy-start(f32[2,4,128]{2,1,0:T(4,128)} %sat_ref.1) | copy-start | bytes 12292
  0.0 1.1 %copy-start.2 = (f32[2,4,128]{2,1,0:T(4,128)S(1)}, f32[2,4,128]{2,1,0:T(4,128)}, u32[]{:S(2)}) copy-start(f32[2,4,128]{2,1,0:T(4,128)} %cour_ref.1) | copy-start | bytes 12292
  0.0 1.2 %copy-start.3 = (f32[4,33]{1,0:T(4,128)S(1)}, f32[4,33]{1,0:T(4,128)}, u32[]{:S(2)}) copy-start(f32[4,33]{1,0:T(4,128)} %rate_ref.1) | copy-start | bytes 1588
  0.0 1.2 %copy-start.4 = (f32[4,33]{1,0:T(4,128)S(1)}, f32[4,33]{1,0:T(4,128)}, u32[]{:S(2)}) copy-start(f32[4,33]{1,0:T(4,128)} %fall_ref.1) | copy-start | bytes 1588
  0.0 1.2 %copy-start.5 = (s32[2,128]{1,0:T(2,128)S(1)}, s32[2,128]{1,0:T(2,128)}, u32[]{:S(2)}) copy-start(s32[2,128]{1,0:T(2,128)} %cloudy_ref.1) | copy-start | bytes 3076
where the time goes:
time: 28.3 us; the launch traced here: 28.2 us
  Pallas kernels  26.2 us (93%)
  local copies, waits for them, and re-layouts  1.94 us (7%)
    pallas_call x1, Pallas kernels, body(): pl.pallas_call(functools.partial(kernel, dims), out_shape=jax.ShapeDtypeS...  26.2 us
    unnamed x14, local copies, waits for them, and re-layouts  1.94 us

commit v1 on v0

--- a/solution.py
+++ b/solution.py
@@ -33,6 +33,8 @@
     tail,
     cells,
     gs,
+    rates,
+    falls,
     edge,
     from_left,
     from_right,
@@ -54,8 +56,7 @@
     lane = lax.broadcasted_iota(jnp.int32, (rows, LANES), 1)
     sub = lax.broadcasted_iota(jnp.int32, (rows, LANES), 0)
 
-    edge[...] = jnp.zeros_like(edge)
-    for t in range(types):
+    def fill(t, packed):
         for b in range(blocks):
             for v in range(levels):
                 g = (t * blocks + b) * levels + v
@@ -65,13 +66,11 @@
                 cells[g, bins : bins + 1] = cour_ref[b, v : v + 1, :]
                 cells[g, bins + 1 : bins + 2] = sat_ref[b, v : v + 1, :]
                 cells[g, bins + 2 : bins + 3] = cloudy_ref[b : b + 1, :].astype(F32)
-    packed = jnp.zeros((rows, LANES), F32)
-    for g in range(groups):
-        packed = jnp.where(
-            (lane >= 4 * g) & (lane < 4 * g + 4),
-            pltpu.roll(cells[g], (4 * g + 2) % LANES, 1),
-            packed,
-        )
+                turned = pltpu.roll(cells[g], lax.rem(4 * g + 2, LANES), 1)
+                packed = jnp.where((lane >= 4 * g) & (lane < 4 * g + 4), turned, packed)
+        return packed
+
+    packed = lax.fori_loop(0, types, fill, jnp.zeros((rows, LANES), F32))
     edge[...] = packed
 
     pl.semaphore_wait(barrier, 2)
@@ -94,13 +93,15 @@
         c = lax.broadcasted_iota(jnp.int32, (rows, bins), 1)
         return jnp.sum(jnp.where(r == c, row, 0.0), axis=1, keepdims=True)
 
-    rates = [jnp.broadcast_to(column(rate_ref, t), (rows, LANES)) for t in range(types)]
-    falls = [jnp.broadcast_to(column(fall_ref, t), (rows, LANES)) for t in range(types)]
+    for t in range(types):
+        rates[t] = jnp.broadcast_to(column(rate_ref, t), (rows, LANES))
+        falls[t] = jnp.broadcast_to(column(fall_ref, t), (rows, LANES))
 
     pairs = coll_ref.shape[2]
     whole = pairs // LANES
     lane_b = lax.broadcasted_iota(jnp.int32, (bins, LANES), 1)
-    for t in range(types):
+
+    def coefficients(t, carry):
         tail[...] = jnp.zeros_like(tail)
         if pairs % LANES:
             tail[0:bins, 0 : pairs - whole * LANES] = coll_ref[t, :, whole * LANES : pairs]
@@ -128,6 +129,9 @@
             k_last[i : i + 1] = stack[low:bins]
             first += count
         cm[t, bins * low :] = k_last[...].astype(BF16)
+        return carry
+
+    lax.fori_loop(0, types, coefficients, 0)
 
     def condense(f, r, sat):
         fr = r * f
@@ -161,24 +165,23 @@
         return jnp.concatenate([x] * times, axis=1) if times > 1 else x
 
     per = 2 if levels % 2 == 0 else 1
-    for t in range(types):
-
-        def one_block(b, carry, t=t):
-            base = (t * blocks + b) * levels
-            wet = []
-            for v in range(0, levels, per):
-                f = jnp.concatenate([cells[base + v + p] for p in range(per)], axis=1)
-                g = condense(f, two(rates[t], per), f[bins + 1 : bins + 2])
-                for _ in range(SUB):
-                    g = collide(t, g)
-                w = jnp.where(f[bins + 2 : bins + 3] > 0, g, f)
-                wet += [w[:, p * LANES : (p + 1) * LANES] for p in range(per)]
-            for v in range(levels):
-                above = wet[v + 1] if v + 1 < levels else jnp.zeros_like(wet[v])
-                cells[base + v] = wet[v] + falls[t] * (above - wet[v])
-            return carry
-
-        lax.fori_loop(0, blocks, one_block, 0)
+
+    def one_block(at, carry):
+        t, base = at // blocks, at * levels
+        wet = []
+        for v in range(0, levels, per):
+            f = jnp.concatenate([cells[base + v + p] for p in range(per)], axis=1)
+            g = condense(f, two(rates[t], per), f[bins + 1 : bins + 2])
+            for _ in range(SUB):
+                g = collide(t, g)
+            w = jnp.where(f[bins + 2 : bins + 3] > 0, g, f)
+            wet += [w[:, p * LANES : (p + 1) * LANES] for p in range(per)]
+        for v in range(levels):
+            above = wet[v + 1] if v + 1 < levels else jnp.zeros_like(wet[v])
+            cells[base + v] = wet[v] + falls[t] * (above - wet[v])
+        return carry
+
+    lax.fori_loop(0, types * blocks, one_block, 0)
 
     for copy in copies:
         copy.wait()
@@ -189,48 +192,54 @@
         r = jnp.where(kind == t, rates[t], r)
         v_fall = jnp.where(kind == t, falls[t], v_fall)
     g = condense(f, r, f[bins + 1 : bins + 2])
-    for _ in range(SUB):
-        new = collide(0, g)
-        for t in range(1, types):
-            new = jnp.where(kind == t, collide(t, g), new)
-        g = new
+
+    def one_type(t, new):
+        mine = g
+        for _ in range(SUB):
+            mine = collide(t, mine)
+        return jnp.where(kind == t, mine, new)
+
+    g = lax.fori_loop(0, types, one_type, g)
     w = jnp.where(f[bins + 2 : bins + 3] > 0, g, f)
     above = jnp.where(lane // 4 % levels == levels - 1, 0.0, pltpu.roll(w, LANES - 4, 1))
     ghost = w + v_fall * (above - w)
     edge[...] = ghost
 
     def shifted(g, x, width_lane):
-        near = pltpu.roll(edge[...], (cols - 2 - 4 * g) % LANES, 1)
+        near = pltpu.roll(edge[...], lax.rem(cols + LANES - 2 - 4 * g, LANES), 1)
         m2 = pltpu.roll(jnp.where(width_lane >= cols - 2, near, x), 2, 1)
         m1 = pltpu.roll(jnp.where(width_lane == cols - 1, near, x), 1, 1)
         p1 = pltpu.roll(jnp.where(width_lane == 0, near, x), LANES - 1, 1)
         p2 = pltpu.roll(jnp.where(width_lane < 2, near, x), LANES - 2, 1)
         return m2, m1, p1, p2
 
-    for b in range(blocks):
-        for v in range(levels):
-            coef = None
-            for t in range(types):
-                g = (t * blocks + b) * levels + v
-                x = cells[g]
-                m2, m1, p1, p2 = shifted(g, x, lane)
-                if coef is None:
-                    c = 0.5 * (x[bins : bins + 1] + p1[bins : bins + 1])
-                    d = 0.5 * (x[bins : bins + 1] + m1[bins : bins + 1])
-                    ca, da = jnp.abs(c), jnp.abs(d)
-                    coef = [
-                        jnp.broadcast_to(e * (1.0 / 12.0), (rows, LANES))
-                        for e in (
-                            da - d,
-                            7.0 * d - 3.0 * da - (ca - c),
-                            7.0 * d + 3.0 * da - (7.0 * c - 3.0 * ca),
-                            -d - da - (7.0 * c + 3.0 * ca),
-                            c + ca,
-                        )
-                    ]
-                y = x + coef[2] * x + coef[0] * m2 + coef[1] * m1 + coef[3] * p1 + coef[4] * p2
-                base = ((b * types + t) * bins) * levels + v
-                out_ref[pl.ds(base, bins, stride=levels), :] = y[0:bins]
+    def advect(at, carry):
+        b, v = at // levels, lax.rem(at, levels)
+        coef = None
+        for t in range(types):
+            g = (t * blocks + b) * levels + v
+            x = cells[g]
+            m2, m1, p1, p2 = shifted(g, x, lane)
+            if coef is None:
+                c = 0.5 * (x[bins : bins + 1] + p1[bins : bins + 1])
+                d = 0.5 * (x[bins : bins + 1] + m1[bins : bins + 1])
+                ca, da = jnp.abs(c), jnp.abs(d)
+                coef = [
+                    jnp.broadcast_to(e * (1.0 / 12.0), (rows, LANES))
+                    for e in (
+                        da - d,
+                        7.0 * d - 3.0 * da - (ca - c),
+                        7.0 * d + 3.0 * da - (7.0 * c - 3.0 * ca),
+                        -d - da - (7.0 * c + 3.0 * ca),
+                        c + ca,
+                    )
+                ]
+            y = x + coef[2] * x + coef[0] * m2 + coef[1] * m1 + coef[3] * p1 + coef[4] * p2
+            base = ((b * types + t) * bins) * levels + v
+            out_ref[pl.ds(base, bins, stride=levels), :] = y[0:bins]
+        return carry
+
+    lax.fori_loop(0, per_type, advect, 0)
 
 
 def body(n_y, spectra, collection, growth_rate, fall_speed, supersaturation, courant, cloudy):
@@ -252,6 +261,8 @@
             pltpu.VMEM((rows, LANES), F32),
             pltpu.VMEM((blocks * types * levels, rows, cols), F32),
             pltpu.VMEM((rows, 2 * cols), F32),
+            pltpu.VMEM((types, rows, LANES), F32),
+            pltpu.VMEM((types, rows, LANES), F32),
             pltpu.VMEM((rows, LANES), F32),
             pltpu.VMEM((rows, LANES), F32),
             pltpu.VMEM((rows, LANES), F32),

time: 28.3 us -> 28.4 us (level)
  no operation moved by 1% of the time
where the time goes in v1:
time: 28.4 us; the launch traced here: 28.3 us
  Pallas kernels  26.3 us (93%)
  local copies, waits for them, and re-layouts  1.94 us (7%)
    pallas_call x1, Pallas kernels, body(): pl.pallas_call(functools.partial(kernel, dims), out_shape=jax.ShapeDtypeS...  26.3 us
    unnamed x14, local copies, waits for them, and re-layouts  1.94 us

profile of v1, /device:TPU:0, one launch (start us, length us, event | category | flops | bytes accessed | tf_op | source)
XLA Modules:
  0.0 28.3 jit_solution(6941816229973182781)
XLA Ops:
  0.0 0.0 copy-start
  0.0 0.0 copy-start.1
  0.0 0.0 copy-start.2
  0.0 0.0 copy-start.3
  0.0 0.0 copy-start.4
  0.0 0.0 copy-start.5
  0.0 1.1 %copy.8.coll_ref = f32[4,33,561]{2,1,0:T(8,128)S(1)} copy(f32[4,33,561]{2,0,1:T(4,128)} %param.8) | data formatting | bytes 592416 | tf_op args[1]
  1.1 0.1 copy-done
  1.1 0.0 copy-done.1
  1.2 0.0 copy-done.2
  1.2 0.0 copy-done.3
  1.2 0.0 copy-done.4
  1.2 0.0 copy-done.5
  1.2 26.3 %shard_map.73 = f32[1056,128]{1,0:T(8,128)S(1)} custom-call(f32[1056,128]{1,0:T(8,128)S(1)} %bitcast.3, f32[4,33,561]{2,1,0:T(8,128)S(1)} %copy.8.coll_ref, f32[4,33]{1,0:T(4,128)S(1)} %copy-done.3, f32[4,33]{1,0:T(4,128)S(1)} %copy-done.4, f32[2,4,128]{2,1,0:T(4,128)S(1)} %copy-done.1, f32[2,4,128]{2,1,0:T(4,128)S(1)} %copy-done.2, s32[2,128]{1,0:T(2,128)S(1)} %copy-done.5), custom_call_target="tpu_custom_call" | custom-call | tf_op jit(solution)/shard_map/pallas_call | solution.py:253
  27.5 0.8 %copy.10 = f32[2,4,33,4,128]{4,3,2,1,0:T(4,128)} copy(f32[2,4,33,4,128]{4,3,2,1,0:T(4,128)S(1)} %bitcast.2) | data formatting | bytes 1081344
Async XLA Ops:
  0.0 1.1 %copy-start = (f32[2,4,33,4,128]{4,3,2,1,0:T(4,128)S(1)}, f32[2,4,33,4,128]{4,3,2,1,0:T(4,128)}, u32[]{:S(2)}) copy-start(f32[2,4,33,4,128]{4,3,2,1,0:T(4,128)} %param.7) | copy-start | bytes 1622020
  0.0 1.1 %copy-start.1 = (f32[2,4,128]{2,1,0:T(4,128)S(1)}, f32[2,4,128]{2,1,0:T(4,128)}, u32[]{:S(2)}) copy-start(f32[2,4,128]{2,1,0:T(4,128)} %sat_ref.1) | copy-start | bytes 12292
  0.0 1.1 %copy-start.2 = (f32[2,4,128]{2,1,0:T(4,128)S(1)}, f32[2,4,128]{2,1,0:T(4,128)}, u32[]{:S(2)}) copy-start(f32[2,4,128]{2,1,0:T(4,128)} %cour_ref.1) | copy-start | bytes 12292
  0.0 1.2 %copy-start.3 = (f32[4,33]{1,0:T(4,128)S(1)}, f32[4,33]{1,0:T(4,128)}, u32[]{:S(2)}) copy-start(f32[4,33]{1,0:T(4,128)} %rate_ref.1) | copy-start | bytes 1588
  0.0 1.2 %copy-start.4 = (f32[4,33]{1,0:T(4,128)S(1)}, f32[4,33]{1,0:T(4,128)}, u32[]{:S(2)}) copy-start(f32[4,33]{1,0:T(4,128)} %fall_ref.1) | copy-start | bytes 1588
  0.0 1.2 %copy-start.5 = (s32[2,128]{1,0:T(2,128)S(1)}, s32[2,128]{1,0:T(2,128)}, u32[]{:S(2)}) copy-start(s32[2,128]{1,0:T(2,128)} %cloudy_ref.1) | copy-start | bytes 3076

commit v2 on v1

--- a/solution.py
+++ b/solution.py
@@ -30,7 +30,7 @@
     out_ref,
     cm,
     k_last,
-    tail,
+    raw,
     cells,
     gs,
     rates,
@@ -73,6 +73,54 @@
     packed = lax.fori_loop(0, types, fill, jnp.zeros((rows, LANES), F32))
     edge[...] = packed
 
+    def column(ref, t):
+        row = jnp.broadcast_to(ref[t : t + 1, :], (rows, bins))
+        r = lax.broadcasted_iota(jnp.int32, (rows, bins), 0)
+        c = lax.broadcasted_iota(jnp.int32, (rows, bins), 1)
+        return jnp.sum(jnp.where(r == c, row, 0.0), axis=1, keepdims=True)
+
+    for t in range(types):
+        rates[t] = jnp.broadcast_to(column(rate_ref, t), (rows, LANES))
+        falls[t] = jnp.broadcast_to(column(fall_ref, t), (rows, LANES))
+
+    pairs = coll_ref.shape[2]
+    raw[...] = jnp.zeros_like(raw)
+    k_last[...] = jnp.zeros_like(k_last)
+    sources = []
+    for a in range(raw.shape[0]):
+        width = min(LANES, pairs - a * LANES)
+        for t in range(types):
+            raw[a, t * rows : t * rows + bins, 0:width] = coll_ref[t, :, a * LANES : a * LANES + width]
+        x = raw[a]
+        hi = x.astype(BF16)
+        sources.append(jnp.concatenate([hi, (x - hi.astype(F32)).astype(BF16)], axis=1))
+    across = lax.broadcasted_iota(jnp.int32, (LANES, LANES), 1)
+    down = lax.broadcasted_iota(jnp.int32, (LANES, LANES), 0)
+    part, inner = across // rows, across % rows
+    inner = jnp.where(inner < bins, inner, -1)
+    inner_hi = jnp.where((part == 0) | (part == 2), inner, -1)
+    inner_lo = jnp.where(part == 1, inner, -1)
+    first = 0
+    for i in range(bins):
+        placed = None
+        for a in range(first // LANES, (first + bins - i - 1) // LANES + 1):
+            offset = first - i - a * LANES
+            pick = jnp.concatenate(
+                [
+                    jnp.where((down == j + offset) & (j >= i), 1.0, 0.0).astype(BF16)
+                    for j in (inner_hi, inner_lo)
+                ],
+                axis=0,
+            )
+            product = jnp.dot(sources[a], pick, preferred_element_type=F32)
+            placed = product if placed is None else placed + product
+        for t in range(types):
+            cm[t, i * low : (i + 1) * low] = placed[t * rows : t * rows + low].astype(BF16)
+            k_last[t, i : i + 1] = placed[t * rows + low : t * rows + bins]
+        first += bins - i
+    for t in range(types):
+        cm[t, bins * low :] = k_last[t].astype(BF16)
+
     pl.semaphore_wait(barrier, 2)
     copies = []
     for index, (peer, landing) in enumerate(((right, from_left), (left, from_right))):
@@ -86,52 +134,6 @@
         )
         copy.start()
         copies.append(copy)
-
-    def column(ref, t):
-        row = jnp.broadcast_to(ref[t : t + 1, :], (rows, bins))
-        r = lax.broadcasted_iota(jnp.int32, (rows, bins), 0)
-        c = lax.broadcasted_iota(jnp.int32, (rows, bins), 1)
-        return jnp.sum(jnp.where(r == c, row, 0.0), axis=1, keepdims=True)
-
-    for t in range(types):
-        rates[t] = jnp.broadcast_to(column(rate_ref, t), (rows, LANES))
-        falls[t] = jnp.broadcast_to(column(fall_ref, t), (rows, LANES))
-
-    pairs = coll_ref.shape[2]
-    whole = pairs // LANES
-    lane_b = lax.broadcasted_iota(jnp.int32, (bins, LANES), 1)
-
-    def coefficients(t, carry):
-        tail[...] = jnp.zeros_like(tail)
-        if pairs % LANES:
-            tail[0:bins, 0 : pairs - whole * LANES] = coll_ref[t, :, whole * LANES : pairs]
-        k_last[...] = jnp.zeros_like(k_last)
-
-        def tile(a):
-            if a < whole:
-                return coll_ref[t, :, a * LANES : (a + 1) * LANES]
-            return tail[0:bins]
-
-        first = 0
-        for i in range(bins):
-            count = bins - i
-            a, end = first // LANES, (first + count - 1) // LANES
-            shift = (i - first) % LANES
-            x = pltpu.roll(tile(a), shift, 1) if shift else tile(a)
-            if end > a:
-                split = i + (a + 1) * LANES - first
-                y = pltpu.roll(tile(end), shift, 1) if shift else tile(end)
-                x = jnp.where(lane_b < split, x, y)
-            x = jnp.where((lane_b >= i) & (lane_b < bins), x, 0.0)
-            hi = rounded(x)
-            stack = hi + pltpu.roll(x - hi, rows, 1) + pltpu.roll(hi, 2 * rows, 1)
-            cm[t, i * low : (i + 1) * low] = stack[0:low].astype(BF16)
-            k_last[i : i + 1] = stack[low:bins]
-            first += count
-        cm[t, bins * low :] = k_last[...].astype(BF16)
-        return carry
-
-    lax.fori_loop(0, types, coefficients, 0)
 
     def condense(f, r, sat):
         fr = r * f
@@ -257,8 +259,8 @@
         out_specs=vmem,
         scratch_shapes=[
             pltpu.VMEM((types, bins * low + last, LANES), BF16),
-            pltpu.VMEM((last, LANES), F32),
-            pltpu.VMEM((rows, LANES), F32),
+            pltpu.VMEM((types, last, LANES), F32),
+            pltpu.VMEM((-(-collection.shape[2] // LANES), types * rows, LANES), F32),
             pltpu.VMEM((blocks * types * levels, rows, cols), F32),
             pltpu.VMEM((rows, 2 * cols), F32),
             pltpu.VMEM((types, rows, LANES), F32),

time: 28.4 us -> 19.9 us (0.70)
  Pallas kernels: 26.3 us -> 17.8 us
    pallas_call x1, Pallas kernels: 26.3 us -> 17.8 us  [body(): pl.pallas_call(functools.partial(kernel, dims), out_shape=jax.ShapeDtypeS...]
where the time goes in v2:
time: 19.9 us; the launch traced here: 19.8 us
  Pallas kernels  17.8 us (89%)
  local copies, waits for them, and re-layouts  1.94 us (10%)
    pallas_call x1, Pallas kernels, body(): pl.pallas_call(functools.partial(kernel, dims), out_shape=jax.ShapeDtypeS...  17.8 us
    unnamed x14, local copies, waits for them, and re-layouts  1.94 us

profile of v2, /device:TPU:0, one launch (start us, length us, event | category | flops | bytes accessed | tf_op | source)
XLA Modules:
  0.0 19.8 jit_solution(11223309181444853297)
XLA Ops:
  0.0 0.0 copy-start
  0.0 0.0 copy-start.1
  0.0 0.0 copy-start.2
  0.0 0.0 copy-start.3
  0.0 0.0 copy-start.4
  0.0 0.0 copy-start.5
  0.0 1.1 %copy.8.coll_ref = f32[4,33,561]{2,1,0:T(8,128)S(1)} copy(f32[4,33,561]{2,0,1:T(4,128)} %param.8) | data formatting | bytes 592416 | tf_op args[1]
  1.1 0.1 copy-done
  1.1 0.0 copy-done.1
  1.2 0.0 copy-done.2
  1.2 0.0 copy-done.3
  1.2 0.0 copy-done.4
  1.2 0.0 copy-done.5
  1.2 17.8 %shard_map.73 = f32[1056,128]{1,0:T(8,128)S(1)} custom-call(f32[1056,128]{1,0:T(8,128)S(1)} %bitcast.3, f32[4,33,561]{2,1,0:T(8,128)S(1)} %copy.8.coll_ref, f32[4,33]{1,0:T(4,128)S(1)} %copy-done.3, f32[4,33]{1,0:T(4,128)S(1)} %copy-done.4, f32[2,4,128]{2,1,0:T(4,128)S(1)} %copy-done.1, f32[2,4,128]{2,1,0:T(4,128)S(1)} %copy-done.2, s32[2,128]{1,0:T(2,128)S(1)} %copy-done.5), custom_call_target="tpu_custom_call" | custom-call | tf_op jit(solution)/shard_map/pallas_call | solution.py:255
  19.0 0.8 %copy.10 = f32[2,4,33,4,128]{4,3,2,1,0:T(4,128)} copy(f32[2,4,33,4,128]{4,3,2,1,0:T(4,128)S(1)} %bitcast.2) | data formatting | bytes 1081344
Async XLA Ops:
  0.0 1.1 %copy-start = (f32[2,4,33,4,128]{4,3,2,1,0:T(4,128)S(1)}, f32[2,4,33,4,128]{4,3,2,1,0:T(4,128)}, u32[]{:S(2)}) copy-start(f32[2,4,33,4,128]{4,3,2,1,0:T(4,128)} %param.7) | copy-start | bytes 1622020
  0.0 1.1 %copy-start.1 = (f32[2,4,128]{2,1,0:T(4,128)S(1)}, f32[2,4,128]{2,1,0:T(4,128)}, u32[]{:S(2)}) copy-start(f32[2,4,128]{2,1,0:T(4,128)} %sat_ref.1) | copy-start | bytes 12292
  0.0 1.1 %copy-start.2 = (f32[2,4,128]{2,1,0:T(4,128)S(1)}, f32[2,4,128]{2,1,0:T(4,128)}, u32[]{:S(2)}) copy-start(f32[2,4,128]{2,1,0:T(4,128)} %cour_ref.1) | copy-start | bytes 12292
  0.0 1.2 %copy-start.3 = (f32[4,33]{1,0:T(4,128)S(1)}, f32[4,33]{1,0:T(4,128)}, u32[]{:S(2)}) copy-start(f32[4,33]{1,0:T(4,128)} %rate_ref.1) | copy-start | bytes 1588
  0.0 1.2 %copy-start.4 = (f32[4,33]{1,0:T(4,128)S(1)}, f32[4,33]{1,0:T(4,128)}, u32[]{:S(2)}) copy-start(f32[4,33]{1,0:T(4,128)} %fall_ref.1) | copy-start | bytes 1588
  0.0 1.2 %copy-start.5 = (s32[2,128]{1,0:T(2,128)S(1)}, s32[2,128]{1,0:T(2,128)}, u32[]{:S(2)}) copy-start(s32[2,128]{1,0:T(2,128)} %cloudy_ref.1) | copy-start | bytes 3076

commit v3 on v2

--- a/solution.py
+++ b/solution.py
@@ -9,7 +9,7 @@
 
 SUB = 2
 LANES = 128
-CHUNK = 4
+CHUNK = 2
 F32 = jnp.float32
 BF16 = jnp.bfloat16
 
@@ -121,6 +121,54 @@
     for t in range(types):
         cm[t, bins * low :] = k_last[t].astype(BF16)
 
+    def column(ref, t):
+        row = jnp.broadcast_to(ref[t : t + 1, :], (rows, bins))
+        r = lax.broadcasted_iota(jnp.int32, (rows, bins), 0)
+        c = lax.broadcasted_iota(jnp.int32, (rows, bins), 1)
+        return jnp.sum(jnp.where(r == c, row, 0.0), axis=1, keepdims=True)
+
+    for t in range(types):
+        rates[t] = jnp.broadcast_to(column(rate_ref, t), (rows, LANES))
+        falls[t] = jnp.broadcast_to(column(fall_ref, t), (rows, LANES))
+
+    pairs = coll_ref.shape[2]
+    raw[...] = jnp.zeros_like(raw)
+    k_last[...] = jnp.zeros_like(k_last)
+    sources = []
+    for a in range(raw.shape[0]):
+        width = min(LANES, pairs - a * LANES)
+        for t in range(types):
+            raw[a, t * rows : t * rows + bins, 0:width] = coll_ref[t, :, a * LANES : a * LANES + width]
+        x = raw[a]
+        hi = x.astype(BF16)
+        sources.append(jnp.concatenate([hi, (x - hi.astype(F32)).astype(BF16)], axis=1))
+    across = lax.broadcasted_iota(jnp.int32, (LANES, LANES), 1)
+    down = lax.broadcasted_iota(jnp.int32, (LANES, LANES), 0)
+    part, inner = across // rows, across % rows
+    inner = jnp.where(inner < bins, inner, -1)
+    inner_hi = jnp.where((part == 0) | (part == 2), inner, -1)
+    inner_lo = jnp.where(part == 1, inner, -1)
+    first = 0
+    for i in range(bins):
+        placed = None
+        for a in range(first // LANES, (first + bins - i - 1) // LANES + 1):
+            offset = first - i - a * LANES
+            pick = jnp.concatenate(
+                [
+                    jnp.where((down == j + offset) & (j >= i), 1.0, 0.0).astype(BF16)
+                    for j in (inner_hi, inner_lo)
+                ],
+                axis=0,
+            )
+            product = jnp.dot(sources[a], pick, preferred_element_type=F32)
+            placed = product if placed is None else placed + product
+        for t in range(types):
+            cm[t, i * low : (i + 1) * low] = placed[t * rows : t * rows + low].astype(BF16)
+            k_last[t, i : i + 1] = placed[t * rows + low : t * rows + bins]
+        first += bins - i
+    for t in range(types):
+        cm[t, bins * low :] = k_last[t].astype(BF16)
+
     pl.semaphore_wait(barrier, 2)
     copies = []
     for index, (peer, landing) in enumerate(((right, from_left), (left, from_right))):
@@ -166,7 +214,7 @@
     def two(x, times):
         return jnp.concatenate([x] * times, axis=1) if times > 1 else x
 
-    per = 2 if levels % 2 == 0 else 1
+    per = levels
 
     def one_block(at, carry):
         t, base = at // blocks, at * levels
@@ -183,7 +231,9 @@
             cells[base + v] = wet[v] + falls[t] * (above - wet[v])
         return carry
 
-    lax.fori_loop(0, types * blocks, one_block, 0)
+    early = types * blocks // 4
+    lax.fori_loop(0, early, one_block, 0)
+    lax.fori_loop(early, types * blocks, one_block, 0)
 
     for copy in copies:
         copy.wait()
@@ -201,7 +251,7 @@
             mine = collide(t, mine)
         return jnp.where(kind == t, mine, new)
 
-    g = lax.fori_loop(0, types, one_type, g)
+    g = lax.fori_loop(0, types, one_type, g, unroll=True)
     w = jnp.where(f[bins + 2 : bins + 3] > 0, g, f)
     above = jnp.where(lane // 4 % levels == levels - 1, 0.0, pltpu.roll(w, LANES - 4, 1))
     ghost = w + v_fall * (above - w)
@@ -262,7 +312,7 @@
             pltpu.VMEM((types, last, LANES), F32),
             pltpu.VMEM((-(-collection.shape[2] // LANES), types * rows, LANES), F32),
             pltpu.VMEM((blocks * types * levels, rows, cols), F32),
-            pltpu.VMEM((rows, 2 * cols), F32),
+            pltpu.VMEM((rows, 4 * cols), F32),
             pltpu.VMEM((types, rows, LANES), F32),
             pltpu.VMEM((types, rows, LANES), F32),
             pltpu.VMEM((rows, LANES), F32),

time: 19.9 us -> 18.8 us (0.945)
  Pallas kernels: 17.8 us -> 16.7 us
    pallas_call x1, Pallas kernels: 17.8 us -> 16.7 us  [body(): pl.pallas_call(functools.partial(kernel, dims), out_shape=jax.ShapeDtypeS...]
where the time goes in v3:
time: 18.8 us; the launch traced here: 18.7 us
  Pallas kernels  16.7 us (89%)
  local copies, waits for them, and re-layouts  1.94 us (10%)
    pallas_call x1, Pallas kernels, body(): pl.pallas_call(functools.partial(kernel, dims), out_shape=jax.ShapeDtypeS...  16.7 us
    unnamed x14, local copies, waits for them, and re-layouts  1.94 us

profile of v3, /device:TPU:0, one launch (start us, length us, event | category | flops | bytes accessed | tf_op | source)
XLA Modules:
  0.0 18.7 jit_solution(1728452610320796689)
XLA Ops:
  0.0 0.0 copy-start
  0.0 0.0 copy-start.1
  0.0 0.0 copy-start.2
  0.0 0.0 copy-start.3
  0.0 0.0 copy-start.4
  0.0 0.0 copy-start.5
  0.0 1.1 %copy.8.coll_ref = f32[4,33,561]{2,1,0:T(8,128)S(1)} copy(f32[4,33,561]{2,0,1:T(4,128)} %param.8) | data formatting | bytes 592416 | tf_op args[1]
  1.1 0.1 copy-done
  1.1 0.0 copy-done.1
  1.2 0.0 copy-done.2
  1.2 0.0 copy-done.3
  1.2 0.0 copy-done.4
  1.2 0.0 copy-done.5
  1.2 16.7 %shard_map.73 = f32[1056,128]{1,0:T(8,128)S(1)} custom-call(f32[1056,128]{1,0:T(8,128)S(1)} %bitcast.3, f32[4,33,561]{2,1,0:T(8,128)S(1)} %copy.8.coll_ref, f32[4,33]{1,0:T(4,128)S(1)} %copy-done.3, f32[4,33]{1,0:T(4,128)S(1)} %copy-done.4, f32[2,4,128]{2,1,0:T(4,128)S(1)} %copy-done.1, f32[2,4,128]{2,1,0:T(4,128)S(1)} %copy-done.2, s32[2,128]{1,0:T(2,128)S(1)} %copy-done.5), custom_call_target="tpu_custom_call" | custom-call | tf_op jit(solution)/shard_map/pallas_call | solution.py:305
  17.9 0.8 %copy.10 = f32[2,4,33,4,128]{4,3,2,1,0:T(4,128)} copy(f32[2,4,33,4,128]{4,3,2,1,0:T(4,128)S(1)} %bitcast.2) | data formatting | bytes 1081344
Async XLA Ops:
  0.0 1.1 %copy-start = (f32[2,4,33,4,128]{4,3,2,1,0:T(4,128)S(1)}, f32[2,4,33,4,128]{4,3,2,1,0:T(4,128)}, u32[]{:S(2)}) copy-start(f32[2,4,33,4,128]{4,3,2,1,0:T(4,128)} %param.7) | copy-start | bytes 1622020
  0.0 1.1 %copy-start.1 = (f32[2,4,128]{2,1,0:T(4,128)S(1)}, f32[2,4,128]{2,1,0:T(4,128)}, u32[]{:S(2)}) copy-start(f32[2,4,128]{2,1,0:T(4,128)} %sat_ref.1) | copy-start | bytes 12292
  0.0 1.1 %copy-start.2 = (f32[2,4,128]{2,1,0:T(4,128)S(1)}, f32[2,4,128]{2,1,0:T(4,128)}, u32[]{:S(2)}) copy-start(f32[2,4,128]{2,1,0:T(4,128)} %cour_ref.1) | copy-start | bytes 12292
  0.0 1.2 %copy-start.3 = (f32[4,33]{1,0:T(4,128)S(1)}, f32[4,33]{1,0:T(4,128)}, u32[]{:S(2)}) copy-start(f32[4,33]{1,0:T(4,128)} %rate_ref.1) | copy-start | bytes 1588
  0.0 1.2 %copy-start.4 = (f32[4,33]{1,0:T(4,128)S(1)}, f32[4,33]{1,0:T(4,128)}, u32[]{:S(2)}) copy-start(f32[4,33]{1,0:T(4,128)} %fall_ref.1) | copy-start | bytes 1588
  0.0 1.2 %copy-start.5 = (s32[2,128]{1,0:T(2,128)S(1)}, s32[2,128]{1,0:T(2,128)}, u32[]{:S(2)}) copy-start(s32[2,128]{1,0:T(2,128)} %cloudy_ref.1) | copy-start | bytes 3076
